TPU v7x, 256 devices: a whole 4x4x8 slice. The times are simulated.
256 devices in a mesh: blk: 64 (over y_hi, z, x), grp: 4 (over y_lo, core).
Axes of the slice: x: 4, y: 4 (y_hi: 2, y_lo: 2; y = y_hi * 2 + y_lo), z: 8, core: 2. Of those that a mesh axis runs over, the one named last changes fastest.
Arguments:
- images: bfloat16 [65536, 1152], P(('blk', 'grp')), may hold values from -0.1875 to 0.1875
- captions: bfloat16 [65536, 1152], P(('blk', 'grp')), may hold values from -0.1875 to 0.1875
- labels: int32 [65536], P(('blk', 'grp')), may hold values from 0 to 65535, as said below
- log_scale: float32 [1], replicated, may hold values from 1.6 to 2.4
- logit_bias: float32 [1], replicated, may hold values from -3 to -1
Outputs:
- row_loss: float32 [65536], P(('blk', 'grp'))
- image_grad: float32 [65536, 1152], P(('blk', 'grp'))
- caption_grad: float32 [65536, 1152], P(('blk', 'grp'))
Inputs may be any that keep to these rules, and one draw needn't show every extreme that they name: labels[i] lies in the same block of 1024 rows as i, and within each block the labels are a permutation of that block's rows.
All inputs are finite; a program needn't handle non-finite values.
Results may differ from a plain program's by a relative error of at most 0.0055.
Values may be sent and summed in bfloat16 or wider, within the bound.
A program may use at most 128 MiB of HBM per device.

v0:
```python
import jax
import jax.numpy as jnp
from jax import lax
from jax.sharding import PartitionSpec as P

STEPS = 3


epsilon = 1e-06


def passed_along(value, axis, steps):
    count = lax.axis_size(axis)
    pairs = [(source, (source + steps) % count) for source in range(count)]
    return lax.ppermute(value, axis, pairs)


def normalize(values):
    widened = values.astype(jnp.float32)
    inverse = lax.rsqrt(jnp.sum(widened * widened, -1, keepdims=True) + epsilon)
    return (inverse, widened * inverse)


def unnormalize(inverse, unit_rows, pull):
    return inverse * (pull - unit_rows * jnp.sum(unit_rows * pull, -1, keepdims=True))


def body(images, captions, labels, log_scale, logit_bias):
    row_count = images.shape[0]
    width = images.shape[1]
    group_size = lax.axis_size("grp")
    cycle_size = lax.axis_size("blk")
    cycle_index = lax.axis_index("blk")
    block_rows = row_count * group_size
    logit_scale = jnp.exp(log_scale[0])
    inv_img, img_unit32 = normalize(images)
    inv_cap, cap_unit32 = normalize(captions)
    img_unit = img_unit32.astype(jnp.bfloat16)
    cap_unit = cap_unit32.astype(jnp.bfloat16)
    columns = lax.broadcasted_iota(jnp.int32, (1, block_rows), 1)
    img_pull = jnp.zeros((row_count, width), jnp.float32)
    loss_sum = jnp.zeros((row_count,), jnp.float32)
    carried = jnp.zeros((block_rows, width), jnp.float32)
    text_block = lax.all_gather(cap_unit, "grp", axis=0, tiled=True)
    for cycle_step in range(STEPS):
        if cycle_step > 0:
            text_block = passed_along(text_block, "blk", 1)
        text_start = (cycle_index - cycle_step) % cycle_size * block_rows
        logits = (
            logit_scale
            * lax.dot_general(
                img_unit, text_block, (((1,), (1,)), ((), ())), preferred_element_type=jnp.float32
            )
            + logit_bias[0]
        )
        positive = labels[:, None] == columns + text_start
        signs = jnp.where(positive, 1.0, -1.0).astype(jnp.float32)
        loss_sum = loss_sum + jnp.sum(-jax.nn.log_sigmoid(signs * logits), -1)
        pair_weight = (jax.nn.sigmoid(logits) - positive.astype(jnp.float32)).astype(jnp.bfloat16)
        img_pull = img_pull + jnp.dot(pair_weight, text_block, preferred_element_type=jnp.float32)
        text_term = lax.dot_general(
            pair_weight, img_unit, (((0,), (0,)), ((), ())), preferred_element_type=jnp.float32
        )
        carried = carried + text_term
        if cycle_step < STEPS - 1:
            carried = passed_along(carried, "blk", 1)
    carried = passed_along(carried, "blk", -(STEPS - 1))
    returned = lax.psum_scatter(carried, "grp", scatter_dimension=0, tiled=True)
    row_loss = loss_sum / (STEPS * block_rows)
    image_grad = unnormalize(inv_img, img_unit32, logit_scale * img_pull)
    caption_grad = unnormalize(inv_cap, cap_unit32, logit_scale * returned)
    return (row_loss, image_grad, caption_grad)


def solution(mesh):
    in_specs = (P(("blk", "grp"), None), P(("blk", "grp"), None), P(("blk", "grp")), P(), P())
    out_specs = (P(("blk", "grp")), P(("blk", "grp"), None), P(("blk", "grp"), None))
    return jax.shard_map(body, mesh=mesh, in_specs=in_specs, out_specs=out_specs, check_vma=False)
```

profile of v0, /device:TPU:1, one launch (start us, length us, event | category | flops | bytes accessed | tf_op | source)
XLA Modules:
  0.0 543.2 jit_solution(17775460087656088506)
XLA Ops:
  7.2 0.0 copy-start.1
  7.2 0.0 all-gather.2.cloned.1.call-start
  7.2 1.3 fusion.17
  8.5 2.0 fusion.3
  10.6 0.0 all-gather.2.cloned.1.call-update
  10.6 0.0 reduce-scatter.2.cloned.1.call-start
  10.7 0.0 copy-done.1
  10.7 0.2 fusion.13
  10.9 38.0 %all-gather.2.cloned.1.call-done = bf16[1024,1152]{1,0:T(8,128)(2,1)} async-done(((bf16[256,1152]{1,0:T(8,128)(2,1)}), bf16[1024,1152]{1,0:T(8,128)(2,1)}) %all-gather.2.cloned.1.call-update) | async-done | bytes 2359312 | tf_op jit(solution)/shard_map/all_gather | solution.py:44
  48.8 1.2 collective-permute-start
  51.4 0.0 copy-start.3
  51.4 2.6 fusion.9
  54.0 0.0 copy-done.3
  54.0 0.0 copy-start.6
  54.0 3.2 fusion.38
  57.2 0.0 copy-done.6
  57.2 1.2 collective-permute-start.2
  58.4 49.5 %collective-permute-done = bf16[1024,1152]{1,0:T(8,128)(2,1)S(1)} collective-permute-done((bf16[1024,1152]{1,0:T(8,128)(2,1)}, bf16[1024,1152]{1,0:T(8,128)(2,1)S(1)}, u32[]{:S(2)}, u32[]{:S(2)}) %collective-permute-start) | collective-permute-done | bytes 2359328 | tf_op jit(solution)/shard_map/ppermute | solution.py:15
  107.9 0.0 collective-permute-start.1
  107.9 151.8 %collective-permute-done.1 = bf16[1024,1152]{1,0:T(8,128)(2,1)} collective-permute-done((bf16[1024,1152]{1,0:T(8,128)(2,1)S(1)}, bf16[1024,1152]{1,0:T(8,128)(2,1)}, u32[]{:S(2)}, u32[]{:S(2)}) %collective-permute-start.1) | collective-permute-done | bytes 2359328 | tf_op jit(solution)/shard_map/ppermute | solution.py:15
  259.7 2.6 fusion.7
  262.3 0.0 copy-done.4
  262.4 0.0 copy-start.9
  262.4 0.0 copy-done.7
  262.4 5.0 fusion.31
  267.4 0.0 collective-permute-done.2
  267.4 3.5 convolution_add_fusion
  270.9 0.1 collective-permute-start.3
  271.0 0.0 copy-done.9
  271.0 1.1 fusion.33
  272.1 107.3 %collective-permute-done.3 = f32[1024,1152]{1,0:T(8,128)S(1)} collective-permute-done((f32[1024,1152]{1,0:T(8,128)S(1)}, f32[1024,1152]{1,0:T(8,128)S(1)}, u32[]{:S(2)}, u32[]{:S(2)}) %collective-permute-start.3) | collective-permute-done | bytes 4718624 | tf_op jit(solution)/shard_map/ppermute | solution.py:15
  379.4 0.5 add.141
  379.8 0.3 collective-permute-start.4
  380.1 103.4 %collective-permute-done.4 = f32[1024,1152]{1,0:T(8,128)} collective-permute-done((f32[1024,1152]{1,0:T(8,128)S(1)}, f32[1024,1152]{1,0:T(8,128)}, u32[]{:S(2)}, u32[]{:S(2)}) %collective-permute-start.4) | collective-permute-done | bytes 4718624 | tf_op jit(solution)/shard_map/ppermute | solution.py:15
  483.5 0.0 reduce-scatter.2.cloned.1.call-update
  483.5 1.2 copy-done.8
  484.7 2.7 fusion.40
  487.4 0.6 add_multiply_fusion
  488.0 0.0 copy-done.5
  488.0 1.0 convolution_add_fusion.2
  489.0 0.2 copy-done.10
  489.2 2.7 fusion.10
  491.9 1.3 fusion.12
  493.2 40.2 %reduce-scatter.2.cloned.1.call-done = f32[256,1152]{1,0:T(8,128)} async-done(((f32[1024,1152]{1,0:T(8,128)}), f32[256,1152]{1,0:T(8,128)}) %reduce-scatter.2.cloned.1.call-update) | async-done | bytes 1179664 | tf_op jit(solution)/shard_map/reduce_scatter | solution.py:68
  533.4 0.0 copy-done
  533.4 1.7 fusion.14
  535.1 0.0 copy-done.2
  535.1 1.3 fusion.16
  (11 shorter events, 0.0 us)
Async XLA Ops:
  7.2 3.5 copy-start.1
  7.2 41.7 %all-gather.2.cloned.1.call-start = ((), (), s32[]{:S(2)}) async-start(), calls=%async_computation.1 | async-start | bytes 2949120 | tf_op jit(solution)/shard_map/all_gather | solution.py:44
  10.6 522.8 %reduce-scatter.2.cloned.1.call-start = ((), (), s32[]{:S(2)}) async-start(), calls=%async_computation.2 | async-start | bytes 5898240 | tf_op jit(solution)/shard_map/reduce_scatter | solution.py:68
  48.8 59.1 %collective-permute-start = (bf16[1024,1152]{1,0:T(8,128)(2,1)}, bf16[1024,1152]{1,0:T(8,128)(2,1)S(1)}, u32[]{:S(2)}, u32[]{:S(2)}) collective-permute-start(bf16[1024,1152]{1,0:T(8,128)(2,1)} %all-gather.2.cloned.1.call-done), channel_id=1, source_target_pairs={{0,4},{4,8},{8,12},{12,16},{16,20},{20,24},{24,28},{28,32},{32,36}... | collective-permute-start | bytes 7077896 | tf_op jit(solution)/shard_map/ppermute | solution.py:15
  51.4 2.6 copy-start.3
  54.0 3.2 copy-start.6
  57.2 210.2 %collective-permute-start.2 = (f32[1024,1152]{1,0:T(8,128)}, f32[1024,1152]{1,0:T(8,128)}, u32[]{:S(2)}, u32[]{:S(2)}) collective-permute-start(f32[1024,1152]{1,0:T(8,128)} %fusion.38), channel_id=1, source_target_pairs={{0,4},{4,8},{8,12},{12,16},{16,20},{20,24},{24,28},{28,32},{32,36}... | collective-permute-start | bytes 14155784 | tf_op jit(solution)/shard_map/ppermute | solution.py:15
  107.9 154.4 %copy-start.4 = (bf16[1024,1152]{1,0:T(8,128)(2,1)}, bf16[1024,1152]{1,0:T(8,128)(2,1)S(1)}, u32[]{:S(2)}) copy-start(bf16[1024,1152]{1,0:T(8,128)(2,1)S(1)} %collective-permute-done) | copy-start | bytes 7077892
  107.9 151.8 %collective-permute-start.1 = (bf16[1024,1152]{1,0:T(8,128)(2,1)S(1)}, bf16[1024,1152]{1,0:T(8,128)(2,1)}, u32[]{:S(2)}, u32[]{:S(2)}) collective-permute-start(bf16[1024,1152]{1,0:T(8,128)(2,1)S(1)} %collective-permute-done), channel_id=1, source_target_pairs={{0,4},{4,8},{8,12},{12,16},{16,20},{20,24},{24,28},{28,32},{32,36}... | collective-permute-start | bytes 7077896 | tf_op jit(solution)/shard_map/ppermute | solution.py:15
  259.7 2.7 copy-start.7
  262.4 8.6 %copy-start.9 = (f32[256,1024]{1,0:T(8,128)}, f32[256,1024]{1,0:T(8,128)S(1)}, u32[]{:S(2)}) copy-start(f32[256,1024]{1,0:T(8,128)S(1)} %fusion.7) | copy-start | bytes 3145732
  270.9 108.5 %collective-permute-start.3 = (f32[1024,1152]{1,0:T(8,128)S(1)}, f32[1024,1152]{1,0:T(8,128)S(1)}, u32[]{:S(2)}, u32[]{:S(2)}) collective-permute-start(f32[1024,1152]{1,0:T(8,128)S(1)} %convolution_add_fusion), channel_id=1, source_target_pairs={{0,4},{4,8},{8,12},{12,16},{16,20},{20,24},{24,28},{28,32},{32,36}... | collective-permute-start | bytes 14155784 | tf_op jit(solution)/shard_map/ppermute | solution.py:15
  379.8 103.6 %collective-permute-start.4 = (f32[1024,1152]{1,0:T(8,128)S(1)}, f32[1024,1152]{1,0:T(8,128)}, u32[]{:S(2)}, u32[]{:S(2)}) collective-permute-start(f32[1024,1152]{1,0:T(8,128)S(1)} %add.141), channel_id=1, source_target_pairs={{0,248},{4,252},{8,0},{12,4},{16,8},{20,12},{24,16},{28,20},{32,24... | collective-permute-start | bytes 14155784 | tf_op jit(solution)/shard_map/ppermute | solution.py:15
  483.5 1.2 copy-start.8
  484.7 3.3 copy-start.5
  488.0 1.2 copy-start.10
  491.9 41.5 %copy-start = (bf16[256,1152]{1,0:T(8,128)(2,1)S(1)}, bf16[256,1152]{1,0:T(8,128)(2,1)}, u32[]{:S(2)}) copy-start(bf16[256,1152]{1,0:T(8,128)(2,1)} %param.6) | copy-start | bytes 1769476
  533.4 1.7 copy-start.2
Sparse Core Ops, SparseCore 0:
  10.7 38.0 all-gather.1
  483.6 49.7 reduce-scatter.1
where the time goes:
time: 544 us; the launch traced here: 543 us
  waiting for transfers between devices  490 us (90%)
  matrix products  24.5 us (5%)
  between operations  15.6 us (3%)
  other arithmetic  8.87 us (2%)
    ppermute x5, waiting for transfers between devices, passed_along(): return lax.ppermute(value, axis, pairs)  412 us
    reduce_scatter x1, waiting for transfers between devices, body(): returned = lax.psum_scatter(carried, 'grp', scatter_dimension=0, tiled=True)  40.2 us
    all_gather x1, waiting for transfers between devices, body(): text_block = lax.all_gather(cap_unit, 'grp', axis=0, tiled=True)  38 us
  transfers between devices with their start and end apart: 7, of which 6 were waited for; matrix products, arithmetic and copies ran while one was open for 4% of the time, Pallas kernels for 0%

commit v1 on v0

v1 whole, which is shorter than its diff:
```python
import jax
import jax.numpy as jnp
from jax import lax
from jax.sharding import PartitionSpec as P

STEPS = 3


epsilon = 1e-06


def passed_along(value, axis, steps):
    count = lax.axis_size(axis)
    pairs = [(source, (source + steps) % count) for source in range(count)]
    return lax.ppermute(value, axis, pairs)


def normalize(values):
    widened = values.astype(jnp.float32)
    inverse = lax.rsqrt(jnp.sum(widened * widened, -1, keepdims=True) + epsilon)
    return (inverse, widened * inverse)


def unnormalize(inverse, unit_rows, pull):
    return inverse * (pull - unit_rows * jnp.sum(unit_rows * pull, -1, keepdims=True))


def body(images, captions, labels, log_scale, logit_bias):
    row_count = images.shape[0]
    group_size = lax.axis_size("grp")
    cycle_index = lax.axis_index("blk")
    member = lax.axis_index("grp")
    block_rows = row_count * group_size
    logit_scale = jnp.exp(log_scale[0])
    inv_img, img_unit32 = normalize(images)
    inv_cap, cap_unit32 = normalize(captions)
    img_unit = img_unit32.astype(jnp.bfloat16)
    cap_unit = cap_unit32.astype(jnp.bfloat16)
    texts = [cap_unit, passed_along(cap_unit, "blk", 1), passed_along(cap_unit, "blk", 2)]
    all_images = lax.all_gather(img_unit, "grp", axis=0, tiled=True)
    all_labels = lax.all_gather(labels, "grp", axis=0, tiled=True)
    rows = lax.broadcasted_iota(jnp.int32, (row_count, 1), 0) + (cycle_index * block_rows + member * row_count)
    loss_sum = jnp.zeros((block_rows,), jnp.float32)
    img_pull = jnp.zeros((block_rows, images.shape[1]), jnp.float32)
    terms = []
    for step in range(STEPS):
        logits = (
            logit_scale
            * lax.dot_general(
                texts[step], all_images, (((1,), (1,)), ((), ())), preferred_element_type=jnp.float32
            )
            + logit_bias[0]
        )
        weight = jax.nn.sigmoid(logits)
        if step == 0:
            positive = all_labels[None, :] == rows
            loss_sum = loss_sum + jnp.sum(-jax.nn.log_sigmoid(jnp.where(positive, logits, -logits)), 0)
            weight = weight - positive.astype(jnp.float32)
        else:
            loss_sum = loss_sum + jnp.sum(-jax.nn.log_sigmoid(-logits), 0)
        weight = weight.astype(jnp.bfloat16)
        terms.append(jnp.dot(weight, all_images, preferred_element_type=jnp.float32))
        img_pull = img_pull + lax.dot_general(
            weight, texts[step], (((0,), (0,)), ((), ())), preferred_element_type=jnp.float32
        )
    cap_pull = terms[0]
    for step in range(1, STEPS):
        cap_pull = cap_pull + passed_along(terms[step].astype(jnp.bfloat16), "blk", -step).astype(jnp.float32)
    own_pull = lax.psum_scatter(img_pull.astype(jnp.bfloat16), "grp", scatter_dimension=0, tiled=True).astype(jnp.float32)
    row_loss = lax.psum_scatter(loss_sum, "grp", scatter_dimension=0, tiled=True) / (STEPS * block_rows)
    image_grad = unnormalize(inv_img, img_unit32, logit_scale * own_pull)
    caption_grad = unnormalize(inv_cap, cap_unit32, logit_scale * cap_pull)
    return (row_loss, image_grad, caption_grad)


def solution(mesh):
    in_specs = (P(("blk", "grp"), None), P(("blk", "grp"), None), P(("blk", "grp")), P(), P())
    out_specs = (P(("blk", "grp")), P(("blk", "grp"), None), P(("blk", "grp"), None))
    return jax.shard_map(body, mesh=mesh, in_specs=in_specs, out_specs=out_specs, check_vma=False)
```

time: 544 us -> 136 us (0.25)
  the two profiles are of different devices: /device:TPU:1 before, /device:TPU:255 now
where the time goes in v1:
time: 136 us
  waiting for transfers between devices  75.8 us (56%)
  matrix products  21.4 us (16%)
  between operations  16.2 us (12%)
  blocking collectives  11.5 us (8%)
  other arithmetic  8.64 us (6%)
  starting transfers between devices  1.69 us (1%)
    ppermute x4, waiting for transfers between devices, passed_along(): return lax.ppermute(value, axis, pairs)  32.8 us
    all_gather x1, waiting for transfers between devices, body(): all_images = lax.all_gather(img_unit, 'grp', axis=0, tiled=True)  26 us
    reduce_scatter x1, waiting for transfers between devices, body(): lax.psum_scatter(img_pull.astype(jnp.bfloat16), 'grp', scatter_dimension=...  17 us
    dot_general x3, matrix products, body(): jnp.dot(weight, all_images, preferred_element_type=jnp.float32)  8.29 us
    dot_general x3, matrix products, body(): lax.dot_general(texts[step], all_images, (((1,), (1,)), ((), ())), prefer...  7.48 us
    all_gather x1, blocking collectives, body(): all_labels = lax.all_gather(labels, 'grp', axis=0, tiled=True)  5.84 us
    unnamed x1, blocking collectives  5.62 us
    dot_general x3, matrix products, body(): lax.dot_general(weight, texts[step], (((0,), (0,)), ((), ())), preferred_...  5.6 us
  transfers between devices with their start and end apart: 6, of which 4 were waited for; matrix products, arithmetic and copies ran while one was open for 14% of the time, Pallas kernels for 0%

profile of v1, /device:TPU:255, one launch (start us, length us, event | category | flops | bytes accessed | tf_op | source)
XLA Modules:
  0.0 135.8 jit_solution(2278538368209084634)
XLA Ops:
  7.2 0.0 copy-start.1
  7.2 0.0 all-gather.3.cloned.1.call-start
  7.2 1.3 fusion.17
  8.5 2.0 %fusion.3 = bf16[256,1152]{1,0:T(8,128)(2,1)} fusion(bf16[256,1152]{1,0:T(8,128)(2,1)} %param.5, f32[256]{0:T(256)S(1)} %add_rsqrt_fusion), kind=kLoop, calls=%fused_computation.14 | loop fusion | flops 884736 | bytes 1180672 | tf_op jit(solution)/shard_map/convert_element_type | solution.py:37
  10.6 0.0 copy-start.3
  10.6 0.0 all-gather.3.cloned.1.call-update
  10.6 0.0 reduce-scatter.2.cloned.1.call-start
  10.7 0.0 copy-done.1
  10.7 0.2 fusion.13
  10.9 0.2 fusion.6
  11.1 0.1 collective-permute-start
  11.2 0.1 collective-permute-start.1
  12.6 0.0 copy-done.3
  12.6 5.8 %all-gather = s32[4,1,256]{2,1,0:T(1,128)S(1)} all-gather(s32[1,1,256]{2,1,0:T(1,128)S(1)} %bitcast.23), channel_id=1, replica_groups=mesh['blk'=64,'grp'=4] {'grp'}, dimensions={0}, use_global_device_ids=true | all-gather | bytes 5120 | tf_op jit(solution)/shard_map/all_gather | solution.py:41
  18.4 26.0 %all-gather.3.cloned.1.call-done = bf16[1024,1152]{1,0:T(8,128)(2,1)} async-done(((bf16[256,1152]{1,0:T(8,128)(2,1)}), bf16[1024,1152]{1,0:T(8,128)(2,1)}) %all-gather.3.cloned.1.call-update) | async-done | bytes 2359312 | tf_op jit(solution)/shard_map/all_gather | solution.py:40
  44.5 0.0 copy-start.4
  44.5 3.3 %fusion.23 = (f32[1024]{0:T(1024)S(1)}, f32[256,1024]{1,0:T(8,128)S(1)}) fusion(s32[1024]{0:T(1024)S(1)} %bitcast.20, s32[256]{0:T(256)S(1)} %iota_add_fusion, f32[]{:T(128)} %bitcast.17, bf16[256,1152]{1,0:T(8,128)(2,1)S(1)} %fusion.6, bf16[1024,1152]{1,0:T(8,128)(2,1)} %all-gather.3.cloned.1.call-done, f32[]{:T(128)} %bitcast.2), kind=kOutput, calls=%fused_computation.42 | convolution fusion | flops 607386624 | bytes 4006920 | tf_op jit(solution)/shard_map/dot_general | solution.py:49
  47.8 0.0 copy-start.7
  47.8 0.0 collective-permute-done
  47.8 0.0 copy-done.4
  47.8 2.8 %fusion.24 = (f32[1024]{0:T(1024)S(1)}, f32[256,1024]{1,0:T(8,128)S(1)}) fusion(f32[]{:T(128)} %bitcast.19, bf16[256,1152]{1,0:T(8,128)(2,1)} %collective-permute-done, bf16[1024,1152]{1,0:T(8,128)(2,1)S(1)} %copy-done.4, f32[]{:T(128)} %bitcast.2), kind=kOutput, calls=%fused_computation.43 | convolution fusion | flops 606338048 | bytes 4001800 | tf_op jit(solution)/shard_map/dot_general | solution.py:49
  50.6 1.1 fusion.28
  51.7 0.0 copy-done.7
  51.7 0.0 collective-permute-done.1
  51.7 1.4 %fusion.25 = (f32[1024]{0:T(1024)S(1)}, f32[256,1024]{1,0:T(8,128)S(1)}) fusion(f32[]{:T(128)} %bitcast.18, bf16[256,1152]{1,0:T(8,128)(2,1)S(1)} %collective-permute-done.1, bf16[1024,1152]{1,0:T(8,128)(2,1)S(1)} %copy-done.4, f32[]{:T(128)} %bitcast.2), kind=kOutput, calls=%fused_computation.44 | convolution fusion | flops 606338048 | bytes 4001800 | tf_op jit(solution)/shard_map/dot_general | solution.py:49
  53.1 2.1 %convolution_add_fusion.1 = f32[1024,1152]{1,0:T(8,128)S(1)} fusion(f32[1024,1152]{1,0:T(8,128)S(1)} %fusion.28, bf16[256,1152]{1,0:T(8,128)(2,1)} %collective-permute-done, f32[256,1024]{1,0:T(8,128)S(1)} %get-tuple-element.8), kind=kOutput, calls=%fused_computation.1 | convolution fusion | flops 606208000 | bytes 11075584 | tf_op jit(solution)/shard_map/dot_general | solution.py:63
  55.2 2.4 %fusion = bf16[1024,1152]{1,0:T(8,128)(2,1)} fusion(f32[1024,1152]{1,0:T(8,128)S(1)} %convolution_add_fusion.1, bf16[256,1152]{1,0:T(8,128)(2,1)S(1)} %collective-permute-done.1, f32[256,1024]{1,0:T(8,128)S(1)} %get-tuple-element.4), kind=kOutput, calls=%fused_computation.2 | convolution fusion | flops 607387648 | bytes 8716288 | tf_op jit(solution)/shard_map/dot_general | solution.py:63
  57.6 0.0 reduce-scatter.2.cloned.1.call-update
  57.7 0.0 copy-start.5
  57.7 3.5 %convolution_convert_fusion.1 = bf16[256,1152]{1,0:T(8,128)(2,1)} fusion(bf16[1024,1152]{1,0:T(8,128)(2,1)} %all-gather.3.cloned.1.call-done, f32[256,1024]{1,0:T(8,128)S(1)} %get-tuple-element.8), kind=kOutput, calls=%fused_computation.7 | convolution fusion | flops 605323264 | bytes 3997696 | tf_op jit(solution)/shard_map/dot_general | solution.py:62
  61.2 0.6 collective-permute-start.2
  61.8 0.0 copy-done.5
  61.8 1.7 %convolution_convert_fusion = bf16[256,1152]{1,0:T(8,128)(2,1)} fusion(bf16[1024,1152]{1,0:T(8,128)(2,1)S(1)} %copy-done.5, f32[256,1024]{1,0:T(8,128)S(1)} %get-tuple-element.4), kind=kOutput, calls=%fused_computation.6 | convolution fusion | flops 605323264 | bytes 3997696 | tf_op jit(solution)/shard_map/dot_general | solution.py:62
  63.4 0.9 collective-permute-start.3
  64.3 0.0 copy-done.6
  64.3 0.6 dynamic-slice
  65.6 5.6 %all-reduce = f32[1024]{0:T(1024)S(1)} all-reduce(f32[1024]{0:T(1024)S(1)} %add_add_fusion), channel_id=2, replica_groups=mesh['blk'=64,'grp'=4] {'grp'}, use_global_device_ids=true, to_apply=%region_5.6.clone | all-reduce | flops 1024 | bytes 8192
  71.2 0.6 dynamic-slice_multiply_fusion
  71.8 29.3 %collective-permute-done.2 = bf16[256,1152]{1,0:T(8,128)(2,1)S(1)} collective-permute-done((bf16[256,1152]{1,0:T(8,128)(2,1)}, bf16[256,1152]{1,0:T(8,128)(2,1)S(1)}, u32[]{:S(2)}, u32[]{:S(2)}) %collective-permute-start.2) | collective-permute-done | bytes 589856 | tf_op jit(solution)/shard_map/ppermute | solution.py:15
  101.2 3.5 %collective-permute-done.3 = bf16[256,1152]{1,0:T(8,128)(2,1)S(1)} collective-permute-done((bf16[256,1152]{1,0:T(8,128)(2,1)}, bf16[256,1152]{1,0:T(8,128)(2,1)S(1)}, u32[]{:S(2)}, u32[]{:S(2)}) %collective-permute-start.3) | collective-permute-done | bytes 589856 | tf_op jit(solution)/shard_map/ppermute | solution.py:15
  104.6 3.1 %fusion.10 = (f32[256]{0:T(256)S(1)}, f32[256,1152]{1,0:T(8,128)S(1)}) fusion(bf16[256,1152]{1,0:T(8,128)(2,1)S(1)} %copy-done.1, f32[256]{0:T(256)S(1)} %add_rsqrt_fusion.1, bf16[256,1152]{1,0:T(8,128)(2,1)S(1)} %collective-permute-done.3, bf16[256,1152]{1,0:T(8,128)(2,1)S(1)} %collective-permute-done.2, f32[]{:T(128)} %bitcast.2, ...), kind=kOutput, calls=%fused_computation.27 | convolution fusion | flops 608468736 | bytes 6364164 | tf_op jit(solution)/shard_map/dot_general | solution.py:62
  107.7 0.0 copy-start
  107.7 1.4 %fusion.12 = f32[256,1152]{1,0:T(8,128)} fusion(bf16[256,1152]{1,0:T(8,128)(2,1)S(1)} %copy-done.1, f32[256]{0:T(256)S(1)} %get-tuple-element.9, f32[256]{0:T(256)S(1)} %add_rsqrt_fusion.1, bf16[256,1152]{1,0:T(8,128)(2,1)S(1)} %collective-permute-done.3, f32[256,1152]{1,0:T(8,128)S(1)} %get-tuple-element.10, ...), kind=kLoop, calls=%fused_computation.29 | loop fusion | flops 2949120 | bytes 4130820 | tf_op jit(solution)/shard_map/mul | solution.py:25
  109.2 17.0 %reduce-scatter.2.cloned.1.call-done = bf16[256,1152]{1,0:T(8,128)(2,1)} async-done(((bf16[1024,1152]{1,0:T(8,128)(2,1)}), bf16[256,1152]{1,0:T(8,128)(2,1)}) %reduce-scatter.2.cloned.1.call-update) | async-done | bytes 589840 | tf_op jit(solution)/shard_map/reduce_scatter | solution.py:69
  126.1 0.0 copy-done
  126.1 1.5 %fusion.14 = f32[256]{0:T(256)S(1)} fusion(bf16[256,1152]{1,0:T(8,128)(2,1)S(1)} %copy-done, bf16[256,1152]{1,0:T(8,128)(2,1)} %reduce-scatter.2.cloned.1.call-done, f32[]{:T(128)} %bitcast.2, f32[256]{0:T(256)S(1)} %add_rsqrt_fusion), kind=kLoop, calls=%fused_computation.31 | loop fusion | flops 1769216 | bytes 1181700 | tf_op jit(solution)/shard_map/reduce_sum | solution.py:25
  127.6 0.0 copy-done.2
  127.6 1.3 fusion.16
  (6 shorter events, 0.0 us)
Async XLA Ops:
  7.2 3.5 %copy-start.1 = (bf16[256,1152]{1,0:T(8,128)(2,1)S(1)}, bf16[256,1152]{1,0:T(8,128)(2,1)}, u32[]{:S(2)}) copy-start(bf16[256,1152]{1,0:T(8,128)(2,1)} %param.6) | copy-start | bytes 1769476
  7.2 37.3 %all-gather.3.cloned.1.call-start = ((), (), s32[]{:S(2)}) async-start(), calls=%async_computation.1 | async-start | bytes 2949120 | tf_op jit(solution)/shard_map/all_gather | solution.py:40
  10.6 2.0 %copy-start.3 = (s32[256]{0:T(256)S(1)}, s32[256]{0:T(256)}, u32[]{:S(2)}) copy-start(s32[256]{0:T(256)} %param.7) | copy-start | bytes 3076
  10.6 115.5 %reduce-scatter.2.cloned.1.call-start = ((), (), s32[]{:S(2)}) async-start(), calls=%async_computation.2 | async-start | bytes 2949120 | tf_op jit(solution)/shard_map/reduce_scatter | solution.py:69
  11.1 36.7 %collective-permute-start = (bf16[256,1152]{1,0:T(8,128)(2,1)S(1)}, bf16[256,1152]{1,0:T(8,128)(2,1)}, u32[]{:S(2)}, u32[]{:S(2)}) collective-permute-start(bf16[256,1152]{1,0:T(8,128)(2,1)S(1)} %fusion.6), channel_id=1, source_target_pairs={{0,4},{4,8},{8,12},{12,16},{16,20},{20,24},{24,28},{28,32},{32,36}... | collective-permute-start | bytes 1769480 | tf_op jit(solution)/shard_map/ppermute | solution.py:15
  11.2 40.5 %collective-permute-start.1 = (bf16[256,1152]{1,0:T(8,128)(2,1)S(1)}, bf16[256,1152]{1,0:T(8,128)(2,1)S(1)}, u32[]{:S(2)}, u32[]{:S(2)}) collective-permute-start(bf16[256,1152]{1,0:T(8,128)(2,1)S(1)} %fusion.6), channel_id=1, source_target_pairs={{0,8},{4,12},{8,16},{12,20},{16,24},{20,28},{24,32},{28,36},{32,40... | collective-permute-start | bytes 1769480 | tf_op jit(solution)/shard_map/ppermute | solution.py:15
  44.5 3.3 %copy-start.4 = (bf16[1024,1152]{1,0:T(8,128)(2,1)S(1)}, bf16[1024,1152]{1,0:T(8,128)(2,1)}, u32[]{:S(2)}) copy-start(bf16[1024,1152]{1,0:T(8,128)(2,1)} %all-gather.3.cloned.1.call-done) | copy-start | bytes 7077892
  47.8 3.9 %copy-start.7 = (f32[256,1024]{1,0:T(8,128)}, f32[256,1024]{1,0:T(8,128)S(1)}, u32[]{:S(2)}) copy-start(f32[256,1024]{1,0:T(8,128)S(1)} %get-tuple-element.6) | copy-start | bytes 3145732
  57.7 4.1 %copy-start.5 = (bf16[1024,1152]{1,0:T(8,128)(2,1)S(1)}, bf16[1024,1152]{1,0:T(8,128)(2,1)}, u32[]{:S(2)}) copy-start(bf16[1024,1152]{1,0:T(8,128)(2,1)} %all-gather.3.cloned.1.call-done) | copy-start | bytes 7077892
  61.2 3.1 %copy-start.6 = (u32[256]{0:T(256)S(1)}, u32[256]{0:T(256)}, u32[]{:S(2)}) copy-start(u32[256]{0:T(256)} %constant.29) | copy-start | bytes 3076
  61.2 40.0 %collective-permute-start.2 = (bf16[256,1152]{1,0:T(8,128)(2,1)}, bf16[256,1152]{1,0:T(8,128)(2,1)S(1)}, u32[]{:S(2)}, u32[]{:S(2)}) collective-permute-start(bf16[256,1152]{1,0:T(8,128)(2,1)} %convolution_convert_fusion.1), channel_id=1, source_target_pairs={{0,252},{4,0},{8,4},{12,8},{16,12},{20,16},{24,20},{28,24},{32,28}... | collective-permute-start | bytes 1769480 | tf_op jit(solution)/shard_map/ppermute | solution.py:15
  63.4 41.2 %collective-permute-start.3 = (bf16[256,1152]{1,0:T(8,128)(2,1)}, bf16[256,1152]{1,0:T(8,128)(2,1)S(1)}, u32[]{:S(2)}, u32[]{:S(2)}) collective-permute-start(bf16[256,1152]{1,0:T(8,128)(2,1)} %convolution_convert_fusion), channel_id=1, source_target_pairs={{0,248},{4,252},{8,0},{12,4},{16,8},{20,12},{24,16},{28,20},{32,24... | collective-permute-start | bytes 1769480 | tf_op jit(solution)/shard_map/ppermute | solution.py:15
  107.7 18.4 %copy-start = (bf16[256,1152]{1,0:T(8,128)(2,1)S(1)}, bf16[256,1152]{1,0:T(8,128)(2,1)}, u32[]{:S(2)}) copy-start(bf16[256,1152]{1,0:T(8,128)(2,1)} %param.5) | copy-start | bytes 1769476
  126.1 1.5 %copy-start.2 = (bf16[256,1152]{1,0:T(8,128)(2,1)S(1)}, bf16[256,1152]{1,0:T(8,128)(2,1)}, u32[]{:S(2)}) copy-start(bf16[256,1152]{1,0:T(8,128)(2,1)} %reduce-scatter.2.cloned.1.call-done) | copy-start | bytes 1769476
Sparse Core Ops, SparseCore 0:
  10.7 33.6 all-gather.2
  57.8 68.3 reduce-scatter.1

commit v2 on v0

v2 whole, which is shorter than its diff:
```python
import functools

import jax
import jax.numpy as jnp
from jax import lax
from jax.experimental import pallas as pl
from jax.experimental.pallas import tpu as pltpu
from jax.sharding import PartitionSpec as P

STEPS = 3
CHUNK = 128
MIB = 2**20

epsilon = 1e-06

f32 = jnp.float32
bf16 = jnp.bfloat16


def places(axes):
    blk_size, _ = axes
    half = blk_size // 2
    blk = lax.axis_index("blk")
    grp = lax.axis_index("grp")
    chip, core = grp // 2, grp % 2

    def along(steps):
        other = (blk + steps + blk_size) % blk_size
        other_chip = (chip + blk // half + other // half) % 2
        return (other, other_chip * 2 + core)

    return dict(
        core=(blk, chip * 2 + 1 - core),
        pair=(blk, (1 - chip) * 2 + core),
        cross=(blk, (1 - chip) * 2 + 1 - core),
        next1=along(1),
        next2=along(2),
        last1=along(-1),
        last2=along(-2),
    )


def kernel(axes, log_scale_ref, bias_ref, img_ref, cap_ref, lab_ref, loss_ref, dimg_ref, dcap_ref,
           imgs, caps, weights, labs, inv_img, inv_cap, loss_acc, loss_in,
           back1, back2, in1, in2, core_out2, core_in2, core_out0, core_in0, pair_out, pair_in,
           send_sems, recv_sems):
    rows, width = img_ref.shape
    block_rows = 4 * rows
    count = rows // CHUNK
    place = places(axes)
    used = [0]
    started = []

    def copy(source, target, to):
        index = used[0]
        used[0] += 1
        made = pltpu.make_async_remote_copy(
            src_ref=source, dst_ref=target, send_sem=send_sems.at[index], recv_sem=recv_sems.at[index],
            device_id=place[to], device_id_type=pl.DeviceIdType.MESH)
        started.append(made)
        return made

    def chunk(index):
        return pl.ds(index * CHUNK, CHUNK)

    barrier = pltpu.get_barrier_semaphore()
    for to in place.values():
        pl.semaphore_signal(barrier, inc=1, device_id=to, device_id_type=pl.DeviceIdType.MESH)

    scale = jnp.exp(jnp.full((1, 1), log_scale_ref[0], f32))
    bias = bias_ref[0]

    def normalize(source, part, inverse_ref, target):
        wide = source[part, :].astype(f32)
        inverse = lax.rsqrt(jnp.sum(wide * wide, -1, keepdims=True) + epsilon)
        inverse_ref[part, :] = inverse
        target[part, :] = (wide * inverse).astype(bf16)

    for i in range(count):
        normalize(img_ref, chunk(i), inv_img, imgs)
    for i in range(count):
        normalize(cap_ref, chunk(i), inv_cap, caps)

    pl.semaphore_wait(barrier, len(place))

    lab_copies = [copy(lab_ref, labs.at[slot], to) for slot, to in ((1, "core"), (2, "pair"), (3, "cross"))]
    to_core = copy(imgs.at[pl.ds(0, rows)], imgs.at[pl.ds(rows, rows)], "core")
    to_pair = [copy(imgs.at[chunk(i)], imgs.at[pl.ds(2 * rows + i * CHUNK, CHUNK)], "pair") for i in range(count)]
    relays = [copy(imgs.at[pl.ds(2 * rows + i * CHUNK, CHUNK)], imgs.at[pl.ds(3 * rows + i * CHUNK, CHUNK)], "core")
              for i in range(count)]
    ahead = {}
    for i in range(count):
        for step, to in ((2, "next2"), (1, "next1")):
            ahead[step, i] = copy(caps.at[chunk(i)], caps.at[pl.ds(step * rows + i * CHUNK, CHUNK)], to)
    for made in lab_copies:
        made.start()
    to_core.start()
    for i in range(count):
        to_pair[i].start()
        ahead[2, i].start()
        ahead[1, i].start()
    labs[0] = lab_ref[...]

    row_index = lax.broadcasted_iota(jnp.int32, (rows, 1), 0) + (
        lax.axis_index("blk") * block_rows + lax.axis_index("grp") * rows)

    def score(start, size, slot, diagonal=False):
        dots = lax.dot_general(caps[pl.ds(start, size), :], imgs[pl.ds(slot * rows, rows), :],
                               (((1,), (1,)), ((), ())), preferred_element_type=f32)
        logits = scale * dots + bias
        grown = jnp.exp(logits)
        total = 1.0 + grown
        inverse = 1.0 / total
        loss = jnp.log(total) + (grown - (total - 1.0)) * inverse
        weight = grown * inverse
        if diagonal:
            positive = labs[slot] == row_index
            loss = loss - jnp.where(positive, logits, 0.0)
            weight = weight - jnp.where(positive, 1.0, 0.0)
        weights[pl.ds(start, size), pl.ds(slot * rows, rows)] = weight.astype(bf16)
        part = jnp.sum(loss, 0, keepdims=True)
        loss_acc[slot] = part if diagonal else loss_acc[slot] + part

    for made in lab_copies:
        made.wait_recv()
    score(0, rows, 0, True)
    to_core.wait_recv()
    score(0, rows, 1, True)
    for i in range(count):
        to_pair[i].wait_recv()
        relays[i].start()
    score(0, rows, 2, True)
    for i in range(count):
        relays[i].wait_recv()
    score(0, rows, 3, True)

    returns = {}
    for i in range(count):
        for step, to, out, landing in ((2, "last2", back2, in2), (1, "last1", back1, in1)):
            ahead[step, i].wait_recv()
            start = step * rows + i * CHUNK
            for slot in range(4):
                score(start, CHUNK, slot)
            out[chunk(i), :] = jnp.dot(weights[pl.ds(start, CHUNK), :], imgs[...],
                                       preferred_element_type=f32).astype(bf16)
            returns[step, i] = copy(out.at[chunk(i)], landing.at[chunk(i)], to)
            returns[step, i].start()

    loss_copies = [copy(loss_acc.at[slot], loss_in.at[slot - 1], to)
                   for slot, to in ((1, "core"), (2, "pair"), (3, "cross"))]
    for made in loss_copies:
        made.start()

    def image_terms(slot, i):
        return lax.dot_general(weights[:, pl.ds(slot * rows + i * CHUNK, CHUNK)], caps[...],
                               (((0,), (0,)), ((), ())), preferred_element_type=f32)

    core2, core0, pairs = [], [], []
    for i in range(count):
        core_out2[chunk(i), :] = image_terms(3, i).astype(bf16)
        core2.append(copy(core_out2.at[chunk(i)], core_in2.at[chunk(i)], "core"))
        core2[i].start()
    for i in range(count):
        own = image_terms(2, i)
        core2[i].wait_recv()
        pair_out[chunk(i), :] = (own + core_in2[chunk(i), :].astype(f32)).astype(bf16)
        pairs.append(copy(pair_out.at[chunk(i)], pair_in.at[chunk(i)], "pair"))
        pairs[i].start()
    for i in range(count):
        core_out0[chunk(i), :] = image_terms(1, i).astype(bf16)
        core0.append(copy(core_out0.at[chunk(i)], core_in0.at[chunk(i)], "core"))
        core0[i].start()
    for i in range(count):
        dimg_ref[chunk(i), :] = image_terms(0, i)
    for i in range(count):
        dcap_ref[chunk(i), :] = jnp.dot(weights[chunk(i), :], imgs[...], preferred_element_type=f32)
    for i in range(count):
        core0[i].wait_recv()
        dimg_ref[chunk(i), :] = dimg_ref[chunk(i), :] + core_in0[chunk(i), :].astype(f32)

    for made in loss_copies:
        made.wait_recv()
    loss_ref[...] = (loss_acc[0] + loss_in[0] + loss_in[1] + loss_in[2]) / (STEPS * block_rows)

    def unnormalize(source, part, inverse_ref, pull):
        inverse = inverse_ref[part, :]
        unit = source[part, :].astype(f32) * inverse
        pull = scale * pull
        return inverse * (pull - unit * jnp.sum(unit * pull, -1, keepdims=True))

    for i in range(count):
        returns[2, i].wait_recv()
        returns[1, i].wait_recv()
        pull = dcap_ref[chunk(i), :] + in1[chunk(i), :].astype(f32) + in2[chunk(i), :].astype(f32)
        dcap_ref[chunk(i), :] = unnormalize(cap_ref, chunk(i), inv_cap, pull)
    for i in range(count):
        pairs[i].wait_recv()
        pull = dimg_ref[chunk(i), :] + pair_in[chunk(i), :].astype(f32)
        dimg_ref[chunk(i), :] = unnormalize(img_ref, chunk(i), inv_img, pull)
    for made in started:
        made.wait_send()


def body(axes, images, captions, labels, log_scale, logit_bias):
    rows, width = images.shape
    vmem = pl.BlockSpec(memory_space=pltpu.VMEM)
    smem = pl.BlockSpec(memory_space=pltpu.SMEM)
    own = pltpu.VMEM((rows, width), bf16)
    loss, image_grad, caption_grad = pl.pallas_call(
        functools.partial(kernel, axes),
        out_shape=(
            jax.ShapeDtypeStruct((1, rows), f32),
            jax.ShapeDtypeStruct((rows, width), f32),
            jax.ShapeDtypeStruct((rows, width), f32),
        ),
        in_specs=[smem, smem, vmem, vmem, vmem],
        out_specs=(vmem, vmem, vmem),
        scratch_shapes=[
            pltpu.VMEM((4 * rows, width), bf16),
            pltpu.VMEM((STEPS * rows, width), bf16),
            pltpu.VMEM((STEPS * rows, 4 * rows), bf16),
            pltpu.VMEM((4, 1, rows), jnp.int32),
            pltpu.VMEM((rows, 1), f32),
            pltpu.VMEM((rows, 1), f32),
            pltpu.VMEM((4, 1, rows), f32),
            pltpu.VMEM((3, 1, rows), f32),
            own, own, own, own, own, own, own, own, own, own,
            pltpu.SemaphoreType.DMA((40,)),
            pltpu.SemaphoreType.DMA((40,)),
        ],
        compiler_params=pltpu.CompilerParams(
            collective_id=0, has_side_effects=True, vmem_limit_bytes=44 * MIB),
        cost_estimate=pl.CostEstimate(
            flops=2 * 3 * STEPS * rows * 4 * rows * width, bytes_accessed=12 * rows * width,
            transcendentals=2 * STEPS * rows * 4 * rows),
        name="contrast",
    )(log_scale, logit_bias, images, captions, labels.reshape(1, rows))
    return (loss.reshape(rows), image_grad, caption_grad)


def solution(mesh):
    axes = (mesh.shape["blk"], mesh.shape["grp"])
    in_specs = (P(("blk", "grp"), None), P(("blk", "grp"), None), P(("blk", "grp")), P(), P())
    out_specs = (P(("blk", "grp")), P(("blk", "grp"), None), P(("blk", "grp"), None))
    return jax.shard_map(functools.partial(body, axes), mesh=mesh, in_specs=in_specs, out_specs=out_specs, check_vma=False)
```

time: 544 us -> 75.9 us (0.14)
  the two profiles are of different devices: /device:TPU:1 before, /device:TPU:11 now
where the time goes in v2:
time: 75.9 us; the launch traced here: 75.7 us
  Pallas kernels  68.3 us (90%)
  local copies, waits for them, and re-layouts  5.39 us (7%)
  between operations  1.94 us (3%)
    pallas_call x1, Pallas kernels, body(): pl.pallas_call(functools.partial(kernel, axes), out_shape=(jax.ShapeDtype...  68.3 us
    unnamed x9, local copies, waits for them, and re-layouts  5.39 us

profile of v2, /device:TPU:11, one launch (start us, length us, event | category | flops | bytes accessed | tf_op | source)
XLA Modules:
  0.0 75.7 jit_solution(10097166202359598307)
XLA Ops:
  1.9 0.0 copy-start
  1.9 1.1 %copy-done = bf16[256,1152]{1,0:T(8,128)(2,1)S(1)} copy-done((bf16[256,1152]{1,0:T(8,128)(2,1)S(1)}, bf16[256,1152]{1,0:T(8,128)(2,1)}, u32[]{:S(2)}) %copy-start) | copy-done | bytes 589848
  3.0 0.0 copy-start.1
  3.0 1.1 %copy-done.1 = bf16[256,1152]{1,0:T(8,128)(2,1)S(1)} copy-done((bf16[256,1152]{1,0:T(8,128)(2,1)S(1)}, bf16[256,1152]{1,0:T(8,128)(2,1)}, u32[]{:S(2)}) %copy-start.1) | copy-done | bytes 589848
  4.1 0.0 copy-start.2
  4.1 0.7 copy-done.2
  4.7 68.3 %contrast.1 = (f32[1,256]{1,0:T(1,128)S(1)}, f32[256,1152]{1,0:T(8,128)S(1)}, f32[256,1152]{1,0:T(8,128)S(1)}) custom-call(f32[1]{0:T(128)S(6)} %copy.11.log_scale_ref, f32[1]{0:T(128)S(6)} %copy.12.bias_ref, bf16[256,1152]{1,0:T(8,128)(2,1)S(1)} %copy-done, bf16[256,1152]{1,0:T(8,128)(2,1)S(1)} %copy-done.1, s32[1,256]{1,0:T(1,128)S(1)} %bitcast.3), custom_call_target="tpu_custom_call" | custom-call | flops 5435817984 | bytes 3538944 | tf_op jit(solution)/shard_map/contrast/pallas_call | solution.py:209
  73.1 0.6 copy.13
  73.7 1.0 %copy.14 = f32[256,1152]{1,0:T(8,128)} copy(f32[256,1152]{1,0:T(8,128)S(1)} %get-tuple-element.13) | data formatting | bytes 2359296
  74.7 1.0 %copy.15 = f32[256,1152]{1,0:T(8,128)} copy(f32[256,1152]{1,0:T(8,128)S(1)} %get-tuple-element.14) | data formatting | bytes 2359296
Async XLA Ops:
  1.9 1.1 %copy-start = (bf16[256,1152]{1,0:T(8,128)(2,1)S(1)}, bf16[256,1152]{1,0:T(8,128)(2,1)}, u32[]{:S(2)}) copy-start(bf16[256,1152]{1,0:T(8,128)(2,1)} %img_ref.1) | copy-start | bytes 1769476
  3.0 1.1 %copy-start.1 = (bf16[256,1152]{1,0:T(8,128)(2,1)S(1)}, bf16[256,1152]{1,0:T(8,128)(2,1)}, u32[]{:S(2)}) copy-start(bf16[256,1152]{1,0:T(8,128)(2,1)} %cap_ref.1) | copy-start | bytes 1769476
  4.1 0.7 copy-start.2

commit v3 on v2

v3 whole, which is shorter than its diff:
```python
import jax
import jax.numpy as jnp
from jax import lax
from jax.experimental import pallas as pl
from jax.experimental.pallas import tpu as pltpu
from jax.sharding import PartitionSpec as P

STEPS = 3
ROW = 4
MIB = 2**20

epsilon = 1e-06

f32 = jnp.float32
bf16 = jnp.bfloat16


def places():
    blk_size = lax.axis_size("blk")
    half = blk_size // 2
    blk = lax.axis_index("blk")
    grp = lax.axis_index("grp")
    chip, core = grp // 2, grp % 2

    def along(start, steps):
        other = (start + steps + blk_size) % blk_size
        other_chip = (chip + start // half + other // half) % 2
        return (other, other_chip * 2 + core)

    def beside(start, steps):
        return start - start % ROW + (start + steps + ROW) % ROW

    def source(steps, sideways):
        other, member = along(blk, steps)
        return (beside(other, sideways), member)

    targets = dict(
        core=(blk, chip * 2 + 1 - core),
        pair=(blk, (1 - chip) * 2 + core),
        cross=(blk, (1 - chip) * 2 + 1 - core),
        next=along(blk, 1),
        last=along(blk, -1),
        right=(beside(blk, 1), grp),
        left=(beside(blk, -1), grp),
        on=along(beside(blk, 1), 2),
        home=along(beside(blk, -1), -2),
    )
    sources = [targets[name] for name in ("core", "pair", "cross", "next", "last", "right", "left")]
    sources += [source(-2, -1), source(2, 1)]
    return targets, sources


def kernel(log_scale_ref, bias_ref, img_ref, cap_ref, lab_ref, loss_ref, dimg_ref, dcap_ref,
           imgs, caps, weights, labs, inv_img, inv_cap, loss_acc, loss_in, passing, own_terms,
           out_last, out_acc, out_far, acc_out, in_last, in_acc, in_passing, in_home, in_sum,
           core_out2, core_in2, core_out0, core_in0, pair_out, pair_in, send_sems, recv_sems):
    rows, width = img_ref.shape
    block_rows = 4 * rows
    piece, part = rows // 4, rows // 2
    place, sources = places()
    started = []

    def copy(source, target, to):
        index = len(started)
        made = pltpu.make_async_remote_copy(
            src_ref=source, dst_ref=target, send_sem=send_sems.at[index], recv_sem=recv_sems.at[index],
            device_id=place[to], device_id_type=pl.DeviceIdType.MESH)
        started.append(made)
        return made

    barrier = pltpu.get_barrier_semaphore()
    for to in sources:
        pl.semaphore_signal(barrier, inc=1, device_id=to, device_id_type=pl.DeviceIdType.MESH)

    scale = jnp.exp(jnp.full((1, 1), log_scale_ref[0], f32))
    bias = bias_ref[0]

    def normalize(source, span, inverse_ref, target):
        wide = source[span, :].astype(f32)
        inverse = lax.rsqrt(jnp.sum(wide * wide, -1, keepdims=True) + epsilon)
        inverse_ref[span, :] = inverse
        target[span, :] = (wide * inverse).astype(bf16)

    for i in range(2):
        normalize(img_ref, pl.ds(i * part, part), inv_img, imgs)
    for i in range(2):
        normalize(cap_ref, pl.ds(i * part, part), inv_cap, caps)

    pl.semaphore_wait(barrier, len(place))

    def at(ref, start, index, size=piece):
        return ref.at[pl.ds(start + index * size, size)]

    lab_copies = [copy(lab_ref, labs.at[slot], to) for slot, to in ((1, "core"), (2, "pair"), (3, "cross"))]
    to_core = copy(at(imgs, 0, 0, rows), at(imgs, rows, 0, rows), "core")
    to_pair = [copy(at(imgs, 0, i), at(imgs, 2 * rows, i), "pair") for i in range(4)]
    pair_on = [copy(at(imgs, 2 * rows, i), at(imgs, 3 * rows, i), "core") for i in range(4)]
    to_next = [copy(at(caps, 0, i), at(caps, rows, i), "next") for i in range(4)]
    next_on = [copy(at(caps, rows, i), at(caps, 2 * rows, i), "next") for i in range(2)]
    to_left = [copy(at(caps, part, i), at(passing, 0, i), "left") for i in range(2)]
    left_on = [copy(at(passing, 0, i), at(caps, 2 * rows + part, i), "on") for i in range(2)]

    for made in lab_copies:
        made.start()
    to_core.start()
    for i in range(4):
        to_pair[i].start()
        to_next[i].start()
        if i < 2:
            to_left[i].start()
    labs[0] = lab_ref[...]

    row_index = lax.broadcasted_iota(jnp.int32, (rows, 1), 0) + (
        lax.axis_index("blk") * block_rows + lax.axis_index("grp") * rows)
    for slot in range(4):
        loss_acc[slot] = jnp.zeros((1, rows), f32)

    def score(start, size, slot):
        dots = lax.dot_general(caps[pl.ds(start, size), :], imgs[pl.ds(slot * rows, rows), :],
                               (((1,), (1,)), ((), ())), preferred_element_type=f32)
        logits = scale * dots + bias
        grown = jnp.exp(logits)
        total = 1.0 + grown
        inverse = 1.0 / total
        loss = jnp.log(total) + (grown - (total - 1.0)) * inverse
        weight = grown * inverse
        if start < rows:
            positive = labs[slot] == row_index[start:start + size]
            loss = loss - jnp.where(positive, logits, 0.0)
            weight = weight - jnp.where(positive, 1.0, 0.0)
        weights[pl.ds(start, size), pl.ds(slot * rows, rows)] = weight.astype(bf16)
        loss_acc[slot] = loss_acc[slot] + jnp.sum(loss, 0, keepdims=True)

    def caption_terms(start, size):
        return jnp.dot(weights[pl.ds(start, size), :], imgs[...], preferred_element_type=f32)

    def image_terms(slot, i):
        return lax.dot_general(weights[:, pl.ds(slot * rows + i * part, part)], caps[...],
                               (((0,), (0,)), ((), ())), preferred_element_type=f32)

    for made in lab_copies:
        made.wait_recv()
    score(0, rows, 0)
    to_core.wait_recv()
    for i in range(4):
        to_next[i].wait_recv()
        if i < 2:
            next_on[i].start()
            to_left[i].wait_recv()
            left_on[i].start()
        to_pair[i].wait_recv()
        pair_on[i].start()
        if i == 0:
            score(0, rows, 1)
        if i == 1:
            score(rows, part, 0)
            score(rows, part, 1)
        if i == 2:
            left_on[0].wait_recv()
            left_on[1].wait_recv()
            score(2 * rows + part, part, 0)
            score(2 * rows + part, part, 1)
    score(rows + part, part, 0)
    score(rows + part, part, 1)
    score(rows + part, part, 2)
    score(2 * rows + part, part, 2)
    for i in range(4):
        pair_on[i].wait_recv()
    score(rows + part, part, 3)

    out_last[...] = caption_terms(rows + part, part).astype(bf16)
    to_last = copy(out_last, in_last, "last")
    to_last.start()
    score(2 * rows + part, part, 3)
    out_far[...] = caption_terms(2 * rows + part, part).astype(bf16)
    to_right = [copy(at(out_far, 0, i), at(in_passing, 0, i), "right") for i in range(2)]
    right_on = [copy(at(in_passing, 0, i), at(in_home, 0, i), "home") for i in range(2)]
    for made in to_right:
        made.start()
    score(rows, part, 2)
    score(rows, part, 3)
    own_terms[...] = caption_terms(rows, part)
    back = [copy(at(out_acc, 0, i), at(in_acc, 0, i), "last") for i in range(2)]
    for i in range(2):
        next_on[i].wait_recv()
        start = 2 * rows + i * piece
        for slot in range(4):
            score(start, piece, slot)
        out_acc[pl.ds(i * piece, piece), :] = caption_terms(start, piece).astype(bf16)
        back[i].start()
        if i == 0:
            score(0, rows, 2)
            score(0, rows, 3)

    core2 = [copy(at(core_out2, 0, i, part), at(core_in2, 0, i, part), "core") for i in range(2)]
    pairs = [copy(at(pair_out, 0, i, part), at(pair_in, 0, i, part), "pair") for i in range(2)]
    core0 = [copy(at(core_out0, 0, i, part), at(core_in0, 0, i, part), "core") for i in range(2)]
    sums = [copy(at(acc_out, 0, i), at(in_sum, 0, i), "last") for i in range(2)]
    loss_copies = [copy(loss_acc.at[slot], loss_in.at[slot - 1], to)
                   for slot, to in ((1, "core"), (2, "pair"), (3, "cross"))]
    for i in range(2):
        core_out2[pl.ds(i * part, part), :] = image_terms(3, i).astype(bf16)
        core2[i].start()
        own = image_terms(2, i)
        core2[i].wait_recv()
        pair_out[pl.ds(i * part, part), :] = (own + core_in2[pl.ds(i * part, part), :].astype(f32)).astype(bf16)
        pairs[i].start()
        to_right[i].wait_recv()
        right_on[i].start()
    for made in loss_copies:
        made.start()
    for i in range(2):
        back[i].wait_recv()
        span = pl.ds(i * piece, piece)
        acc_out[span, :] = (own_terms[span, :] + in_acc[span, :].astype(f32)).astype(bf16)
        sums[i].start()
        core_out0[pl.ds(i * part, part), :] = image_terms(1, i).astype(bf16)
        core0[i].start()
    for i in range(2):
        dimg_ref[pl.ds(i * part, part), :] = image_terms(0, i)
    for i in range(2):
        dcap_ref[pl.ds(i * part, part), :] = caption_terms(i * part, part)
    for i in range(2):
        core0[i].wait_recv()
        span = pl.ds(i * part, part)
        dimg_ref[span, :] = dimg_ref[span, :] + core_in0[span, :].astype(f32)

    for made in loss_copies:
        made.wait_recv()
    loss_ref[...] = (loss_acc[0] + loss_in[0] + loss_in[1] + loss_in[2]) / (STEPS * block_rows)

    def unnormalize(source, span, inverse_ref, pull):
        inverse = inverse_ref[span, :]
        unit = source[span, :].astype(f32) * inverse
        pull = scale * pull
        return inverse * (pull - unit * jnp.sum(unit * pull, -1, keepdims=True))

    to_last.wait_recv()
    for i in range(2):
        right_on[i].wait_recv()
        span, near = pl.ds(part + i * piece, piece), pl.ds(i * piece, piece)
        pull = dcap_ref[span, :] + in_last[near, :].astype(f32) + in_home[near, :].astype(f32)
        dcap_ref[span, :] = unnormalize(cap_ref, span, inv_cap, pull)
    for i in range(2):
        sums[i].wait_recv()
        span = pl.ds(i * piece, piece)
        pull = dcap_ref[span, :] + in_sum[span, :].astype(f32)
        dcap_ref[span, :] = unnormalize(cap_ref, span, inv_cap, pull)
    for i in range(2):
        pairs[i].wait_recv()
        span = pl.ds(i * part, part)
        pull = dimg_ref[span, :] + pair_in[span, :].astype(f32)
        dimg_ref[span, :] = unnormalize(img_ref, span, inv_img, pull)
    for made in started:
        made.wait_send()


def body(images, captions, labels, log_scale, logit_bias):
    rows, width = images.shape
    vmem = pl.BlockSpec(memory_space=pltpu.VMEM)
    smem = pl.BlockSpec(memory_space=pltpu.SMEM)
    own = pltpu.VMEM((rows, width), bf16)
    half = pltpu.VMEM((rows // 2, width), bf16)
    loss, image_grad, caption_grad = pl.pallas_call(
        kernel,
        out_shape=(
            jax.ShapeDtypeStruct((1, rows), f32),
            jax.ShapeDtypeStruct((rows, width), f32),
            jax.ShapeDtypeStruct((rows, width), f32),
        ),
        in_specs=[smem, smem, vmem, vmem, vmem],
        out_specs=(vmem, vmem, vmem),
        scratch_shapes=[
            pltpu.VMEM((4 * rows, width), bf16),
            pltpu.VMEM((STEPS * rows, width), bf16),
            pltpu.VMEM((STEPS * rows, 4 * rows), bf16),
            pltpu.VMEM((4, 1, rows), jnp.int32),
            pltpu.VMEM((rows, 1), f32),
            pltpu.VMEM((rows, 1), f32),
            pltpu.VMEM((4, 1, rows), f32),
            pltpu.VMEM((3, 1, rows), f32),
            half, pltpu.VMEM((rows // 2, width), f32),
            half, half, half, half, half, half, half, half, half,
            own, own, own, own, own, own,
            pltpu.SemaphoreType.DMA((40,)),
            pltpu.SemaphoreType.DMA((40,)),
        ],
        compiler_params=pltpu.CompilerParams(
            collective_id=0, has_side_effects=True, vmem_limit_bytes=44 * MIB),
        cost_estimate=pl.CostEstimate(
            flops=2 * 3 * STEPS * rows * 4 * rows * width, bytes_accessed=12 * rows * width,
            transcendentals=2 * STEPS * rows * 4 * rows),
        name="contrast",
    )(log_scale, logit_bias, images, captions, labels.reshape(1, rows))
    return (loss.reshape(rows), image_grad, caption_grad)


def solution(mesh):
    in_specs = (P(("blk", "grp"), None), P(("blk", "grp"), None), P(("blk", "grp")), P(), P())
    out_specs = (P(("blk", "grp")), P(("blk", "grp"), None), P(("blk", "grp"), None))
    return jax.shard_map(body, mesh=mesh, in_specs=in_specs, out_specs=out_specs, check_vma=False)
```

time: 75.9 us -> 69 us (0.909)
  the two profiles are of different devices: /device:TPU:11 before, /device:TPU:1 now
where the time goes in v3:
time: 69 us; the launch traced here: 68.8 us
  Pallas kernels  61.4 us (89%)
  local copies, waits for them, and re-layouts  5.39 us (8%)
  between operations  1.94 us (3%)
    pallas_call x1, Pallas kernels, body(): pl.pallas_call(kernel, out_shape=(jax.ShapeDtypeStruct((1, rows), f32), j...  61.4 us
    unnamed x9, local copies, waits for them, and re-layouts  5.39 us

profile of v3, /device:TPU:1, one launch (start us, length us, event | category | flops | bytes accessed | tf_op | source)
XLA Modules:
  0.0 68.8 jit_solution(7086378153809777547)
XLA Ops:
  1.9 0.0 copy-start
  1.9 1.1 %copy-done = bf16[256,1152]{1,0:T(8,128)(2,1)S(1)} copy-done((bf16[256,1152]{1,0:T(8,128)(2,1)S(1)}, bf16[256,1152]{1,0:T(8,128)(2,1)}, u32[]{:S(2)}) %copy-start) | copy-done | bytes 589848
  3.0 0.0 copy-start.1
  3.0 1.1 %copy-done.1 = bf16[256,1152]{1,0:T(8,128)(2,1)S(1)} copy-done((bf16[256,1152]{1,0:T(8,128)(2,1)S(1)}, bf16[256,1152]{1,0:T(8,128)(2,1)}, u32[]{:S(2)}) %copy-start.1) | copy-done | bytes 589848
  4.1 0.0 copy-start.2
  4.1 0.7 copy-done.2
  4.7 61.4 %contrast.1 = (f32[1,256]{1,0:T(1,128)S(1)}, f32[256,1152]{1,0:T(8,128)S(1)}, f32[256,1152]{1,0:T(8,128)S(1)}) custom-call(f32[1]{0:T(128)S(6)} %copy.11.log_scale_ref, f32[1]{0:T(128)S(6)} %copy.12.bias_ref, bf16[256,1152]{1,0:T(8,128)(2,1)S(1)} %copy-done, bf16[256,1152]{1,0:T(8,128)(2,1)S(1)} %copy-done.1, s32[1,256]{1,0:T(1,128)S(1)} %bitcast.3), custom_call_target="tpu_custom_call" | custom-call | flops 5435817984 | bytes 3538944 | tf_op jit(solution)/shard_map/contrast/pallas_call | solution.py:264
  66.2 0.6 copy.13
  66.7 1.0 %copy.14 = f32[256,1152]{1,0:T(8,128)} copy(f32[256,1152]{1,0:T(8,128)S(1)} %get-tuple-element.13) | data formatting | bytes 2359296
  67.8 1.0 %copy.15 = f32[256,1152]{1,0:T(8,128)} copy(f32[256,1152]{1,0:T(8,128)S(1)} %get-tuple-element.14) | data formatting | bytes 2359296
Async XLA Ops:
  1.9 1.1 %copy-start = (bf16[256,1152]{1,0:T(8,128)(2,1)S(1)}, bf16[256,1152]{1,0:T(8,128)(2,1)}, u32[]{:S(2)}) copy-start(bf16[256,1152]{1,0:T(8,128)(2,1)} %img_ref.1) | copy-start | bytes 1769476
  3.0 1.1 %copy-start.1 = (bf16[256,1152]{1,0:T(8,128)(2,1)S(1)}, bf16[256,1152]{1,0:T(8,128)(2,1)}, u32[]{:S(2)}) copy-start(bf16[256,1152]{1,0:T(8,128)(2,1)} %cap_ref.1) | copy-start | bytes 1769476
  4.1 0.7 copy-start.2

commit v4 on v3

--- a/solution.py
+++ b/solution.py
@@ -30,31 +30,47 @@
     def beside(start, steps):
         return start - start % ROW + (start + steps + ROW) % ROW
 
-    def source(steps, sideways):
-        other, member = along(blk, steps)
-        return (beside(other, sideways), member)
-
+    def crosses(start, steps):
+        return (start // half + (start + steps + blk_size) % blk_size // half) % 2
+
+    def side(start, steps):
+        change = crosses(start, 2 * steps)
+        return (beside(start, -steps) + change * half) % blk_size, change
+
+    def served(start, steps):
+        other = beside(start, steps)
+        change = crosses(other, 2 * steps)
+        return (other + change * half) % blk_size, change
+
+    def member(change):
+        return (chip + change) % 2 * 2 + core
+
+    left, left_change = side(blk, 1)
+    right, right_change = side(blk, -1)
+    from_right, from_right_change = served(blk, 1)
+    from_left, from_left_change = served(blk, -1)
     targets = dict(
         core=(blk, chip * 2 + 1 - core),
         pair=(blk, (1 - chip) * 2 + core),
         cross=(blk, (1 - chip) * 2 + 1 - core),
         next=along(blk, 1),
         last=along(blk, -1),
-        right=(beside(blk, 1), grp),
-        left=(beside(blk, -1), grp),
-        on=along(beside(blk, 1), 2),
-        home=along(beside(blk, -1), -2),
+        left=(left, member(left_change)),
+        right=(right, member(right_change)),
+        on=((from_right + 2) % blk_size, grp),
+        home=((from_left - 2 + blk_size) % blk_size, grp),
     )
-    sources = [targets[name] for name in ("core", "pair", "cross", "next", "last", "right", "left")]
-    sources += [source(-2, -1), source(2, 1)]
+    sources = [targets[name] for name in ("core", "pair", "cross", "next", "last")]
+    sources += [(from_right, member(from_right_change)), (from_left, member(from_left_change))]
+    sources += [(side((blk - 2 + blk_size) % blk_size, 1)[0], grp), (side((blk + 2) % blk_size, -1)[0], grp)]
     return targets, sources
 
 
-def kernel(log_scale_ref, bias_ref, img_ref, cap_ref, lab_ref, loss_ref, dimg_ref, dcap_ref,
-           imgs, caps, weights, labs, inv_img, inv_cap, loss_acc, loss_in, passing, own_terms,
+def kernel(log_scale_ref, bias_ref, img_hbm, cap_hbm, lab_hbm, loss_ref, dimg_ref, dcap_ref,
+           img_ref, cap_ref, lab_ref, load_sems, imgs, caps, weights, labs, inv_img, inv_cap, loss_acc, loss_in, passing, own_terms,
            out_last, out_acc, out_far, acc_out, in_last, in_acc, in_passing, in_home, in_sum,
            core_out2, core_in2, core_out0, core_in0, pair_out, pair_in, send_sems, recv_sems):
-    rows, width = img_ref.shape
+    rows, width = dimg_ref.shape
     block_rows = 4 * rows
     piece, part = rows // 4, rows // 2
     place, sources = places()
@@ -72,6 +88,10 @@
     for to in sources:
         pl.semaphore_signal(barrier, inc=1, device_id=to, device_id_type=pl.DeviceIdType.MESH)
 
+    loads = [pltpu.make_async_copy(source, target, load_sems.at[i])
+             for i, (source, target) in enumerate(((img_hbm, img_ref), (cap_hbm, cap_ref), (lab_hbm, lab_ref)))]
+    for made in loads:
+        made.start()
     scale = jnp.exp(jnp.full((1, 1), log_scale_ref[0], f32))
     bias = bias_ref[0]
 
@@ -81,11 +101,14 @@
         inverse_ref[span, :] = inverse
         target[span, :] = (wide * inverse).astype(bf16)
 
+    loads[0].wait()
     for i in range(2):
         normalize(img_ref, pl.ds(i * part, part), inv_img, imgs)
+    loads[1].wait()
     for i in range(2):
         normalize(cap_ref, pl.ds(i * part, part), inv_cap, caps)
 
+    loads[2].wait()
     pl.semaphore_wait(barrier, len(place))
 
     def at(ref, start, index, size=piece):
@@ -258,6 +281,7 @@
 def body(images, captions, labels, log_scale, logit_bias):
     rows, width = images.shape
     vmem = pl.BlockSpec(memory_space=pltpu.VMEM)
+    hbm = pl.BlockSpec(memory_space=pltpu.HBM)
     smem = pl.BlockSpec(memory_space=pltpu.SMEM)
     own = pltpu.VMEM((rows, width), bf16)
     half = pltpu.VMEM((rows // 2, width), bf16)
@@ -268,9 +292,10 @@
             jax.ShapeDtypeStruct((rows, width), f32),
             jax.ShapeDtypeStruct((rows, width), f32),
         ),
-        in_specs=[smem, smem, vmem, vmem, vmem],
+        in_specs=[smem, smem, hbm, hbm, hbm],
         out_specs=(vmem, vmem, vmem),
         scratch_shapes=[
+            own, own, pltpu.VMEM((1, rows), jnp.int32), pltpu.SemaphoreType.DMA((3,)),
             pltpu.VMEM((4 * rows, width), bf16),
             pltpu.VMEM((STEPS * rows, width), bf16),
             pltpu.VMEM((STEPS * rows, 4 * rows), bf16),

time: 69 us -> 63.9 us (0.926)
  Pallas kernels: 61.4 us -> 56.3 us
    pallas_call x1, Pallas kernels: 61.4 us -> 56.3 us  [body(): pl.pallas_call(kernel, out_shape=(jax.ShapeDtypeStruct((1, rows), f32), j...]
where the time goes in v4:
time: 63.9 us; the launch traced here: 63.7 us
  Pallas kernels  56.3 us (88%)
  local copies, waits for them, and re-layouts  5.39 us (8%)
  between operations  1.94 us (3%)
    pallas_call x1, Pallas kernels, body(): pl.pallas_call(kernel, out_shape=(jax.ShapeDtypeStruct((1, rows), f32), j...  56.3 us
    unnamed x9, local copies, waits for them, and re-layouts  5.39 us

profile of v4, /device:TPU:1, one launch (start us, length us, event | category | flops | bytes accessed | tf_op | source)
XLA Modules:
  0.0 63.7 jit_solution(6605853870388981489)
XLA Ops:
  1.9 0.0 copy-start
  1.9 1.1 %copy-done = bf16[256,1152]{1,0:T(8,128)(2,1)S(1)} copy-done((bf16[256,1152]{1,0:T(8,128)(2,1)S(1)}, bf16[256,1152]{1,0:T(8,128)(2,1)}, u32[]{:S(2)}) %copy-start) | copy-done | bytes 589848
  3.0 0.0 copy-start.1
  3.0 1.1 %copy-done.1 = bf16[256,1152]{1,0:T(8,128)(2,1)S(1)} copy-done((bf16[256,1152]{1,0:T(8,128)(2,1)S(1)}, bf16[256,1152]{1,0:T(8,128)(2,1)}, u32[]{:S(2)}) %copy-start.1) | copy-done | bytes 589848
  4.1 0.0 copy-start.2
  4.1 0.7 %copy-done.2 = s32[256]{0:T(256)S(1)} copy-done((s32[256]{0:T(256)S(1)}, s32[256]{0:T(256)}, u32[]{:S(2)}) %copy-start.2) | copy-done | bytes 1048
  4.7 56.3 %contrast.1 = (f32[1,256]{1,0:T(1,128)S(1)}, f32[256,1152]{1,0:T(8,128)S(1)}, f32[256,1152]{1,0:T(8,128)S(1)}) custom-call(f32[1]{0:T(128)S(6)} %copy.11.log_scale_ref, f32[1]{0:T(128)S(6)} %copy.12.bias_ref, bf16[256,1152]{1,0:T(8,128)(2,1)S(1)} %copy-done, bf16[256,1152]{1,0:T(8,128)(2,1)S(1)} %copy-done.1, s32[1,256]{1,0:T(1,128)S(1)} %bitcast.3), custom_call_target="tpu_custom_call" | custom-call | flops 5435817984 | bytes 3538944 | tf_op jit(solution)/shard_map/contrast/pallas_call | solution.py:288
  61.1 0.6 copy.13
  61.6 1.0 %copy.14 = f32[256,1152]{1,0:T(8,128)} copy(f32[256,1152]{1,0:T(8,128)S(1)} %get-tuple-element.13) | data formatting | bytes 2359296
  62.6 1.0 %copy.15 = f32[256,1152]{1,0:T(8,128)} copy(f32[256,1152]{1,0:T(8,128)S(1)} %get-tuple-element.14) | data formatting | bytes 2359296
Async XLA Ops:
  1.9 1.1 %copy-start = (bf16[256,1152]{1,0:T(8,128)(2,1)S(1)}, bf16[256,1152]{1,0:T(8,128)(2,1)}, u32[]{:S(2)}) copy-start(bf16[256,1152]{1,0:T(8,128)(2,1)} %img_hbm.1) | copy-start | bytes 1769476
  3.0 1.1 %copy-start.1 = (bf16[256,1152]{1,0:T(8,128)(2,1)S(1)}, bf16[256,1152]{1,0:T(8,128)(2,1)}, u32[]{:S(2)}) copy-start(bf16[256,1152]{1,0:T(8,128)(2,1)} %cap_hbm.1) | copy-start | bytes 1769476
  4.1 0.7 %copy-start.2 = (s32[256]{0:T(256)S(1)}, s32[256]{0:T(256)}, u32[]{:S(2)}) copy-start(s32[256]{0:T(256)} %param.7) | copy-start | bytes 3076

commit v5 on v4

--- a/solution.py
+++ b/solution.py
@@ -278,6 +278,19 @@
         made.wait_send()
 
 
+def store(loss_ref, dimg_ref, dcap_ref, loss_hbm, dimg_hbm, dcap_hbm, sems):
+    pieces = []
+    for source, target in ((dimg_ref, dimg_hbm), (dcap_ref, dcap_hbm)):
+        size = source.shape[0] // 4
+        pieces += [(source.at[pl.ds(i * size, size)], target.at[pl.ds(i * size, size)]) for i in range(4)]
+    pieces.append((loss_ref, loss_hbm))
+    copies = [pltpu.make_async_copy(source, target, sems.at[i]) for i, (source, target) in enumerate(pieces)]
+    for made in copies:
+        made.start()
+    for made in copies:
+        made.wait()
+
+
 def body(images, captions, labels, log_scale, logit_bias):
     rows, width = images.shape
     vmem = pl.BlockSpec(memory_space=pltpu.VMEM)
@@ -288,9 +301,9 @@
     loss, image_grad, caption_grad = pl.pallas_call(
         kernel,
         out_shape=(
-            jax.ShapeDtypeStruct((1, rows), f32),
-            jax.ShapeDtypeStruct((rows, width), f32),
-            jax.ShapeDtypeStruct((rows, width), f32),
+            pltpu.VMEM((1, rows), f32),
+            pltpu.VMEM((rows, width), f32),
+            pltpu.VMEM((rows, width), f32),
         ),
         in_specs=[smem, smem, hbm, hbm, hbm],
         out_specs=(vmem, vmem, vmem),
@@ -316,7 +329,21 @@
             flops=2 * 3 * STEPS * rows * 4 * rows * width, bytes_accessed=12 * rows * width,
             transcendentals=2 * STEPS * rows * 4 * rows),
         name="contrast",
-    )(log_scale, logit_bias, images, captions, labels.reshape(1, rows))
+    )(log_scale, logit_bias, *(pltpu.with_memory_space_constraint(value, pltpu.HBM)
+                               for value in (images, captions, labels.reshape(1, rows))))
+    loss, image_grad, caption_grad = pl.pallas_call(
+        store,
+        out_shape=(
+            jax.ShapeDtypeStruct((1, rows), f32),
+            jax.ShapeDtypeStruct((rows, width), f32),
+            jax.ShapeDtypeStruct((rows, width), f32),
+        ),
+        in_specs=[vmem, vmem, vmem],
+        out_specs=(hbm, hbm, hbm),
+        scratch_shapes=[pltpu.SemaphoreType.DMA((9,))],
+        compiler_params=pltpu.CompilerParams(vmem_limit_bytes=4 * MIB),
+        name="store",
+    )(loss, image_grad, caption_grad)
     return (loss.reshape(rows), image_grad, caption_grad)
 
 

time: 63.9 us -> 60.1 us (0.941)
  local copies, waits for them, and re-layouts: 5.39 us -> 0 us
  Pallas kernels: 56.3 us -> 58 us
    unnamed x9 -> x0, local copies, waits for them, and re-layouts: 5.39 us -> none
    pallas_call x1 -> x2, Pallas kernels: 56.3 us -> 58 us  [the longest x1 56.5 us: body(): pl.pallas_call(kernel, out_shape=(pltpu.VMEM((1, rows), f32), pltpu.VMEM(...]
where the time goes in v5:
time: 60.1 us; the launch traced here: 59.9 us
  Pallas kernels  58 us (97%)
  between operations  1.93 us (3%)
    pallas_call x1, Pallas kernels, body(): pl.pallas_call(kernel, out_shape=(pltpu.VMEM((1, rows), f32), pltpu.VMEM(...  56.5 us
    pallas_call x1, Pallas kernels, body(): pl.pallas_call(store, out_shape=(jax.ShapeDtypeStruct((1, rows), f32), ja...  1.48 us

profile of v5, /device:TPU:1, one launch (start us, length us, event | category | flops | bytes accessed | tf_op | source)
XLA Modules:
  0.0 59.9 jit_solution(13227507987148390263)
XLA Ops:
  1.9 56.5 %contrast.1 = (f32[1,256]{1,0:T(1,128)S(1)}, f32[256,1152]{1,0:T(8,128)S(1)}, f32[256,1152]{1,0:T(8,128)S(1)}) custom-call(f32[1]{0:T(128)S(6)} %copy.8.log_scale_ref, f32[1]{0:T(128)S(6)} %copy.9.bias_ref, bf16[256,1152]{1,0:T(8,128)(2,1)} %img_hbm.1, bf16[256,1152]{1,0:T(8,128)(2,1)} %cap_hbm.1, s32[1,256]{1,0:T(1,128)} %bitcast.2), custom_call_target="tpu_custom_call" | custom-call | flops 5435817984 | bytes 3538944 | tf_op jit(solution)/shard_map/contrast/pallas_call | solution.py:301
  58.5 1.5 %store.1 = (f32[1,256]{1,0:T(1,128)}, f32[256,1152]{1,0:T(8,128)}, f32[256,1152]{1,0:T(8,128)}) custom-call(f32[1,256]{1,0:T(1,128)S(1)} %get-tuple-element.9.loss_ref, f32[256,1152]{1,0:T(8,128)S(1)} %get-tuple-element.10.dimg_ref, f32[256,1152]{1,0:T(8,128)S(1)} %get-tuple-element.11.dcap_ref), custom_call_target="tpu_custom_call" | custom-call | tf_op jit(solution)/shard_map/store/pallas_call | solution.py:334

commit v6 on v5

--- a/solution.py
+++ b/solution.py
@@ -166,13 +166,14 @@
     score(0, rows, 0)
     to_core.wait_recv()
     for i in range(4):
+        to_pair[i].wait_recv()
+        pair_on[i].start()
+        if i < 2:
+            to_left[i].wait_recv()
+            left_on[i].start()
         to_next[i].wait_recv()
         if i < 2:
             next_on[i].start()
-            to_left[i].wait_recv()
-            left_on[i].start()
-        to_pair[i].wait_recv()
-        pair_on[i].start()
         if i == 0:
             score(0, rows, 1)
         if i == 1:
@@ -187,6 +188,8 @@
     score(rows + part, part, 1)
     score(rows + part, part, 2)
     score(2 * rows + part, part, 2)
+    score(rows, part, 2)
+    score(0, rows, 2)
     for i in range(4):
         pair_on[i].wait_recv()
     score(rows + part, part, 3)
@@ -200,20 +203,17 @@
     right_on = [copy(at(in_passing, 0, i), at(in_home, 0, i), "home") for i in range(2)]
     for made in to_right:
         made.start()
-    score(rows, part, 2)
     score(rows, part, 3)
-    own_terms[...] = caption_terms(rows, part)
+    score(0, rows, 3)
     back = [copy(at(out_acc, 0, i), at(in_acc, 0, i), "last") for i in range(2)]
     for i in range(2):
         next_on[i].wait_recv()
         start = 2 * rows + i * piece
         for slot in range(4):
             score(start, piece, slot)
-        out_acc[pl.ds(i * piece, piece), :] = caption_terms(start, piece).astype(bf16)
-        back[i].start()
         if i == 0:
-            score(0, rows, 2)
-            score(0, rows, 3)
+            out_acc[pl.ds(0, piece), :] = caption_terms(start, piece).astype(bf16)
+            back[0].start()
 
     core2 = [copy(at(core_out2, 0, i, part), at(core_in2, 0, i, part), "core") for i in range(2)]
     pairs = [copy(at(pair_out, 0, i, part), at(pair_in, 0, i, part), "pair") for i in range(2)]
@@ -224,12 +224,16 @@
     for i in range(2):
         core_out2[pl.ds(i * part, part), :] = image_terms(3, i).astype(bf16)
         core2[i].start()
+        if i == 0:
+            out_acc[pl.ds(piece, piece), :] = caption_terms(2 * rows + piece, piece).astype(bf16)
+            back[1].start()
         own = image_terms(2, i)
         core2[i].wait_recv()
         pair_out[pl.ds(i * part, part), :] = (own + core_in2[pl.ds(i * part, part), :].astype(f32)).astype(bf16)
         pairs[i].start()
         to_right[i].wait_recv()
         right_on[i].start()
+    own_terms[...] = caption_terms(rows, part)
     for made in loss_copies:
         made.start()
     for i in range(2):

time: 60.1 us -> 59 us (0.982)
  Pallas kernels: 58 us -> 56.9 us
    pallas_call x1, Pallas kernels: 56.5 us -> 55.5 us  [body(): pl.pallas_call(kernel, out_shape=(pltpu.VMEM((1, rows), f32), pltpu.VMEM(...]
where the time goes in v6:
time: 59 us; the launch traced here: 58.9 us
  Pallas kernels  56.9 us (96%)
  between operations  1.93 us (3%)
    pallas_call x1, Pallas kernels, body(): pl.pallas_call(kernel, out_shape=(pltpu.VMEM((1, rows), f32), pltpu.VMEM(...  55.5 us
    pallas_call x1, Pallas kernels, body(): pl.pallas_call(store, out_shape=(jax.ShapeDtypeStruct((1, rows), f32), ja...  1.48 us

profile of v6, /device:TPU:1, one launch (start us, length us, event | category | flops | bytes accessed | tf_op | source)
XLA Modules:
  0.0 58.9 jit_solution(13640768405573834143)
XLA Ops:
  1.9 55.5 %contrast.1 = (f32[1,256]{1,0:T(1,128)S(1)}, f32[256,1152]{1,0:T(8,128)S(1)}, f32[256,1152]{1,0:T(8,128)S(1)}) custom-call(f32[1]{0:T(128)S(6)} %copy.8.log_scale_ref, f32[1]{0:T(128)S(6)} %copy.9.bias_ref, bf16[256,1152]{1,0:T(8,128)(2,1)} %img_hbm.1, bf16[256,1152]{1,0:T(8,128)(2,1)} %cap_hbm.1, s32[1,256]{1,0:T(1,128)} %bitcast.2), custom_call_target="tpu_custom_call" | custom-call | flops 5435817984 | bytes 3538944 | tf_op jit(solution)/shard_map/contrast/pallas_call | solution.py:305
  57.4 1.5 %store.1 = (f32[1,256]{1,0:T(1,128)}, f32[256,1152]{1,0:T(8,128)}, f32[256,1152]{1,0:T(8,128)}) custom-call(f32[1,256]{1,0:T(1,128)S(1)} %get-tuple-element.9.loss_ref, f32[256,1152]{1,0:T(8,128)S(1)} %get-tuple-element.10.dimg_ref, f32[256,1152]{1,0:T(8,128)S(1)} %get-tuple-element.11.dcap_ref), custom_call_target="tpu_custom_call" | custom-call | tf_op jit(solution)/shard_map/store/pallas_call | solution.py:338

commit v7 on v6

--- a/solution.py
+++ b/solution.py
@@ -123,14 +123,15 @@
     to_left = [copy(at(caps, part, i), at(passing, 0, i), "left") for i in range(2)]
     left_on = [copy(at(passing, 0, i), at(caps, 2 * rows + part, i), "on") for i in range(2)]
 
-    for made in lab_copies:
-        made.start()
-    to_core.start()
     for i in range(4):
-        to_pair[i].start()
         to_next[i].start()
         if i < 2:
             to_left[i].start()
+        to_pair[i].start()
+        if i == 0:
+            to_core.start()
+            for made in lab_copies:
+                made.start()
     labs[0] = lab_ref[...]
 
     row_index = lax.broadcasted_iota(jnp.int32, (rows, 1), 0) + (
@@ -224,10 +225,10 @@
     for i in range(2):
         core_out2[pl.ds(i * part, part), :] = image_terms(3, i).astype(bf16)
         core2[i].start()
+        own = image_terms(2, i)
         if i == 0:
             out_acc[pl.ds(piece, piece), :] = caption_terms(2 * rows + piece, piece).astype(bf16)
             back[1].start()
-        own = image_terms(2, i)
         core2[i].wait_recv()
         pair_out[pl.ds(i * part, part), :] = (own + core_in2[pl.ds(i * part, part), :].astype(f32)).astype(bf16)
         pairs[i].start()

time: 59 us -> 55.2 us (0.936)
  Pallas kernels: 56.9 us -> 53.2 us
    pallas_call x1, Pallas kernels: 55.5 us -> 51.7 us  [body(): pl.pallas_call(kernel, out_shape=(pltpu.VMEM((1, rows), f32), pltpu.VMEM(...]
where the time goes in v7:
time: 55.2 us; the launch traced here: 55.1 us
  Pallas kernels  53.2 us (96%)
  between operations  1.93 us (3%)
    pallas_call x1, Pallas kernels, body(): pl.pallas_call(kernel, out_shape=(pltpu.VMEM((1, rows), f32), pltpu.VMEM(...  51.7 us
    pallas_call x1, Pallas kernels, body(): pl.pallas_call(store, out_shape=(jax.ShapeDtypeStruct((1, rows), f32), ja...  1.48 us

profile of v7, /device:TPU:1, one launch (start us, length us, event | category | flops | bytes accessed | tf_op | source)
XLA Modules:
  0.0 55.1 jit_solution(4912440618492401341)
XLA Ops:
  1.9 51.7 %contrast.1 = (f32[1,256]{1,0:T(1,128)S(1)}, f32[256,1152]{1,0:T(8,128)S(1)}, f32[256,1152]{1,0:T(8,128)S(1)}) custom-call(f32[1]{0:T(128)S(6)} %copy.8.log_scale_ref, f32[1]{0:T(128)S(6)} %copy.9.bias_ref, bf16[256,1152]{1,0:T(8,128)(2,1)} %img_hbm.1, bf16[256,1152]{1,0:T(8,128)(2,1)} %cap_hbm.1, s32[1,256]{1,0:T(1,128)} %bitcast.2), custom_call_target="tpu_custom_call" | custom-call | flops 5435817984 | bytes 3538944 | tf_op jit(solution)/shard_map/contrast/pallas_call | solution.py:306
  53.6 1.5 %store.1 = (f32[1,256]{1,0:T(1,128)}, f32[256,1152]{1,0:T(8,128)}, f32[256,1152]{1,0:T(8,128)}) custom-call(f32[1,256]{1,0:T(1,128)S(1)} %get-tuple-element.9.loss_ref, f32[256,1152]{1,0:T(8,128)S(1)} %get-tuple-element.10.dimg_ref, f32[256,1152]{1,0:T(8,128)S(1)} %get-tuple-element.11.dcap_ref), custom_call_target="tpu_custom_call" | custom-call | tf_op jit(solution)/shard_map/store/pallas_call | solution.py:339
